TPU v7x, 256 devices: a whole 4x4x8 slice. The times are simulated.
256 devices in a mesh: wide: 16 (over y, z_lo), narrow: 16 (over x, z_hi, core).
Axes of the slice: x: 4, y: 4, z: 8 (z_hi: 2, z_lo: 4; z = z_hi * 4 + z_lo), core: 2. Of those that a mesh axis runs over, the one named last changes fastest.
Arguments:
- residual: float32 [16, 16, 6, 192, 512], P('wide', 'narrow'), may hold values from -6 to 6
- face_schur: float32 [16, 16, 6, 192, 192], P('wide', 'narrow'), may hold values from -0.5 to 1.5, as said below
- local_solver: bfloat16 [16, 16, 1152, 1152], P('wide', 'narrow'), may hold values from -0.1875 to 0.1875
- interface_functional_set: float32 [3, 192, 16], replicated, may hold values from -0.4375 to 0.4375
- coarse_inverse: float32 [12288, 12288], P('wide', 'narrow'), may hold values from -0.109375 to 0.109375
Outputs:
- preconditioned: float32 [16, 16, 3, 192, 512], P('wide', 'narrow')
Inputs may be any that keep to these rules, and one draw needn't show every extreme that they name: `face_schur`: every face block is symmetric positive definite.
All inputs are finite; a program needn't handle non-finite values. Where the computation divides by a largest or mean magnitude, that divisor is 1e-20 or more.
Results may differ from a plain program's by a relative error of at most 0.002.
Values sent between devices are 32-bit elements; how exact they have to be, the bound alone decides.
A program may use at most 64 MiB of HBM per device.

v0:
```python
import jax
import jax.numpy as jnp
from jax import lax
from jax.sharding import PartitionSpec as P

NS_STEPS = 12


exact_arithmetic_mode = lax.Precision.HIGHEST


def extended(block, sides, width):
    for axis, dim in sides:
        count = lax.axis_size(axis)
        forward = [(i, i + 1) for i in range(count - 1)]
        forward.append((count - 1, 0))
        backward = [(target, source) for source, target in forward]
        low = lax.ppermute(
            lax.slice_in_dim(block, block.shape[dim] - width, None, axis=dim), axis, forward
        )
        high = lax.ppermute(lax.slice_in_dim(block, 0, width, axis=dim), axis, backward)
        block = jnp.concatenate([low, block, high], axis=dim)
    return block


def passed_along(value, axis, steps):
    count = lax.axis_size(axis)
    pairs = [(source, (source + steps) % count) for source in range(count)]
    return lax.ppermute(value, axis, pairs)


def newton_schulz(matrices):
    row_sums = jnp.max(jnp.sum(jnp.abs(matrices), axis=2), axis=1)
    approx = matrices / (row_sums * row_sums)[:, None, None]
    for iteration in range(NS_STEPS):
        product = jnp.einsum("bij,bjk->bik", matrices, approx, precision=exact_arithmetic_mode)
        approx = 2.0 * approx - jnp.einsum(
            "bij,bjk->bik", approx, product, precision=exact_arithmetic_mode
        )
    return approx


def apply_faces(blocks, fields):
    return jnp.einsum("fij,fjr->fir", blocks, fields, precision=exact_arithmetic_mode)


def per_device(residual, face_schur, local_solver, interface_functional_set, coarse_inverse):
    blocks = face_schur[0, 0]
    face_loads = residual[0, 0]
    face_order = blocks.shape[1]
    columns_count = face_loads.shape[2]
    wide_joined = jnp.concatenate([blocks[0:2], face_loads[0:2]], axis=2)
    wide_padded = extended(wide_joined, (("wide", 0),), 1)
    narrow_joined = jnp.concatenate([blocks[2:4], face_loads[2:4]], axis=2)
    slim_side_extended = extended(narrow_joined, (("narrow", 0),), 1)
    face_sums = jnp.stack(
        [
            wide_padded[0, :, :face_order] + blocks[0],
            blocks[1] + wide_padded[3, :, :face_order],
            slim_side_extended[0, :, :face_order] + blocks[2],
            blocks[3] + slim_side_extended[3, :, :face_order],
            blocks[4] + blocks[5],
        ],
        axis=0,
    )
    assembled_vector = jnp.stack(
        [
            wide_padded[0, :, face_order:] + face_loads[0],
            face_loads[1] + wide_padded[3, :, face_order:],
            slim_side_extended[0, :, face_order:] + face_loads[2],
            face_loads[3] + slim_side_extended[3, :, face_order:],
            face_loads[4] + face_loads[5],
        ],
        axis=0,
    )
    owned_values = jnp.stack(
        [assembled_vector[1], assembled_vector[3], assembled_vector[4]], axis=0
    )
    inverse = newton_schulz(face_sums)
    scaled = apply_faces(inverse, assembled_vector)
    face_scaled = jnp.concatenate([scaled, scaled[4:5]], axis=0)
    owned_inverse = jnp.stack([inverse[1], inverse[3], inverse[4]], axis=0)
    restricted_residual = jnp.einsum(
        "psk,pse->pke", interface_functional_set, owned_values, precision=exact_arithmetic_mode
    )
    restricted_residual = restricted_residual.reshape(-1, columns_count)
    incomplete_total = jnp.dot(
        coarse_inverse,
        lax.all_gather(restricted_residual, "wide", axis=0, tiled=True),
        precision=exact_arithmetic_mode,
        preferred_element_type=jnp.float32,
    )
    own_rows = restricted_residual.shape[0]
    summed = lax.psum(incomplete_total, "narrow")
    own_coarse = lax.dynamic_slice_in_dim(summed, lax.axis_index("narrow") * own_rows, own_rows, 0)
    local_loads = apply_faces(blocks, face_scaled).astype(jnp.bfloat16)
    flattened = local_loads.reshape(-1, columns_count)
    solved = jnp.dot(local_solver[0, 0], flattened, preferred_element_type=jnp.float32)
    solved = solved.reshape(6, face_order, columns_count)
    weighted = apply_faces(blocks, solved)
    wide_back = passed_along(weighted[0], "wide", -1)
    narrow_back = passed_along(weighted[2], "narrow", -1)
    combined = jnp.stack(
        [weighted[1] + wide_back, weighted[3] + narrow_back, weighted[4] + weighted[5]], axis=0
    )
    local_part = apply_faces(owned_inverse, combined)
    update_increment = own_coarse.reshape(3, -1, columns_count)
    coarse_component = jnp.einsum(
        "fek,fkg->feg", interface_functional_set, update_increment, precision=exact_arithmetic_mode
    )
    output_answer = local_part + coarse_component
    return output_answer[None, None]


def solution(mesh):
    placed = (
        P("wide", "narrow", None, None, None),
        P("wide", "narrow", None, None, None),
        P("wide", "narrow", None, None),
        P(),
        P("wide", "narrow"),
    )
    return jax.shard_map(
        per_device,
        mesh=mesh,
        in_specs=placed,
        out_specs=P("wide", "narrow", None, None, None),
        check_vma=False,
    )
```

profile of v0, /device:TPU:65, one launch (start us, length us, event | category | flops | bytes accessed | tf_op | source)
XLA Modules:
  0.0 394.8 jit_solution(18344340595628974362)
XLA Ops:
  6.5 1.6 slice_bitcast_fusion
  8.2 0.2 copy-done.4
  8.5 0.3 pad_maximum_fusion.1
  8.8 1.7 collective-permute-start
  10.5 0.3 pad_maximum_fusion
  10.8 6.1 %collective-permute-start.2 = (f32[1,192,704]{2,1,0:T(8,128)S(1)}, f32[1,192,704]{2,1,0:T(8,128)S(1)}, u32[]{:S(2)}, u32[]{:S(2)}) collective-permute-start(f32[1,192,704]{2,1,0:T(8,128)S(1)} %get-tuple-element.19), channel_id=1, source_target_pairs={{0,1},{1,2},{2,3},{3,4},{4,5},{5,6},{6,7},{7,8},{8,9},{9,10},{10,1... | collective-permute-start | bytes 1622024 | tf_op jit(solution)/shard_map/ppermute | solution.py:18
  17.0 0.5 collective-permute-start.3
  17.5 6.0 %collective-permute-done = f32[1,192,704]{2,1,0:T(8,128)S(1)} collective-permute-done((f32[1,192,704]{2,1,0:T(8,128)S(1)}, f32[1,192,704]{2,1,0:T(8,128)S(1)}, u32[]{:S(2)}, u32[]{:S(2)}) %collective-permute-start) | collective-permute-done | bytes 540704 | tf_op jit(solution)/shard_map/ppermute | solution.py:18
  23.6 12.8 %collective-permute-done.1 = f32[1,192,704]{2,1,0:T(8,128)S(1)} collective-permute-done((f32[1,192,704]{2,1,0:T(8,128)S(1)}, f32[1,192,704]{2,1,0:T(8,128)S(1)}, u32[]{:S(2)}, u32[]{:S(2)}) %collective-permute-start.1) | collective-permute-done | bytes 540704 | tf_op jit(solution)/shard_map/ppermute | solution.py:21
  36.4 24.0 %collective-permute-done.2 = f32[1,192,704]{2,1,0:T(8,128)S(1)} collective-permute-done((f32[1,192,704]{2,1,0:T(8,128)S(1)}, f32[1,192,704]{2,1,0:T(8,128)S(1)}, u32[]{:S(2)}, u32[]{:S(2)}) %collective-permute-start.2) | collective-permute-done | bytes 540704 | tf_op jit(solution)/shard_map/ppermute | solution.py:18
  60.5 6.1 %collective-permute-done.3 = f32[1,192,704]{2,1,0:T(8,128)S(1)} collective-permute-done((f32[1,192,704]{2,1,0:T(8,128)S(1)}, f32[1,192,704]{2,1,0:T(8,128)S(1)}, u32[]{:S(2)}, u32[]{:S(2)}) %collective-permute-start.3) | collective-permute-done | bytes 540704 | tf_op jit(solution)/shard_map/ppermute | solution.py:21
  66.6 0.7 copy-done.16
  67.4 0.9 copy-done.1
  68.3 0.2 abs_reduce_fusion
  68.7 2.8 fusion.22
  71.5 1.2 convolution_subtract_fusion.11
  72.7 1.1 fusion.45
  73.8 1.1 convolution_subtract_fusion.10
  74.9 1.1 fusion.46
  76.0 1.1 convolution_subtract_fusion.9
  77.1 1.1 fusion.47
  78.2 1.1 convolution_subtract_fusion.8
  79.3 1.1 fusion.48
  80.4 1.1 convolution_subtract_fusion.7
  81.5 1.3 fusion.49
  82.8 1.1 convolution_subtract_fusion.6
  83.9 1.1 fusion.50
  85.0 1.1 convolution_subtract_fusion.5
  86.1 1.1 fusion.51
  87.3 2.1 convolution_subtract_fusion.4
  89.5 0.2 constant_dynamic-update-slice_fusion.2
  89.7 0.7 copy-done.15
  90.4 0.2 fusion.36
  90.6 0.2 constant_dynamic-update-slice_fusion.1
  90.8 1.3 copy-done.10
  92.1 1.4 fusion.14
  93.5 0.3 all-reduce.2.cloned.1.call-start
  93.8 2.7 fusion.52
  96.5 1.1 convolution_subtract_fusion.3
  97.7 1.1 fusion.53
  98.8 1.1 convolution_subtract_fusion.2
  99.9 1.1 fusion.54
  101.0 1.1 convolution_subtract_fusion.1
  102.1 1.1 fusion.55
  103.2 1.1 convolution_subtract_fusion
  104.3 0.4 copy-done.11
  104.7 1.8 fusion.56
  106.6 3.8 fusion.5
  110.4 53.5 %all-gather.2.cloned.1.call-done = f32[768,512]{1,0:T(8,128)} async-done(((f32[48,512]{1,0:T(8,128)}), f32[768,512]{1,0:T(8,128)}) %all-gather.2.cloned.1.call-update) | async-done | bytes 1572880 | tf_op jit(solution)/shard_map/all_gather | solution.py:89
  163.9 10.8 %convolution_bitcast_fusion.2 = f32[768,512]{0,1:T(8,128)} fusion(f32[768,512]{1,0:T(8,128)} %all-gather.2.cloned.1.call-done, f32[768,768]{1,0:T(8,128)} %param.9), kind=kOutput, calls=%fused_computation.8 | convolution fusion | flops 3623878656 | bytes 5505024 | tf_op jit(solution)/shard_map/dot_general | solution.py:87
  174.8 4.6 %convolution_bitcast_fusion = f32[1152,512]{0,1:T(8,128)} fusion(bf16[1152,512]{1,0:T(8,128)(2,1)} %bitcast.133, bf16[1,1,1152,1152]{3,2,1,0:T(8,128)(2,1)S(1)} %copy-done), kind=kOutput, calls=%fused_computation | convolution fusion | flops 1358954496 | bytes 6193152 | tf_op jit(solution)/shard_map/dot_general | solution.py:98
  179.3 3.2 copy.9
  182.6 4.3 %convolution_bitcast_fusion.1 = f32[6,192,512]{2,1,0:T(8,128)S(1)} fusion(f32[6,192,512]{2,1,0:T(8,128)} %bitcast.132, f32[1,1,6,192,192]{4,3,2,1,0:T(8,128)} %param.6), kind=kOutput, calls=%fused_computation.6 | convolution fusion | flops 1358954496 | bytes 5603328 | tf_op jit(solution)/shard_map/fij,fjr->fir/dot_general | solution.py:44
  186.9 1.4 copy-done.6
  188.3 1.1 slice_bitcast_fusion.4
  189.4 4.0 %collective-permute-start.4 = (f32[192,512]{1,0:T(8,128)}, f32[192,512]{1,0:T(8,128)}, u32[]{:S(2)}, u32[]{:S(2)}) collective-permute-start(f32[192,512]{1,0:T(8,128)} %get-tuple-element.13), channel_id=1, source_target_pairs={{0,240},{16,0},{32,16},{48,32},{64,48},{80,64},{96,80},{112,96},{1... | collective-permute-start | bytes 1179656 | tf_op jit(solution)/shard_map/ppermute | solution.py:29
  193.4 11.4 %collective-permute-start.5 = (f32[192,512]{1,0:T(8,128)}, f32[192,512]{1,0:T(8,128)}, u32[]{:S(2)}, u32[]{:S(2)}) collective-permute-start(f32[192,512]{1,0:T(8,128)} %get-tuple-element.15), channel_id=1, source_target_pairs={{0,15},{1,0},{2,1},{3,2},{4,3},{5,4},{6,5},{7,6},{8,7},{9,8},{10,9... | collective-permute-start | bytes 1179656 | tf_op jit(solution)/shard_map/ppermute | solution.py:29
  204.8 11.1 %collective-permute-done.5 = f32[192,512]{1,0:T(8,128)} collective-permute-done((f32[192,512]{1,0:T(8,128)}, f32[192,512]{1,0:T(8,128)}, u32[]{:S(2)}, u32[]{:S(2)}) %collective-permute-start.5) | collective-permute-done | bytes 393248 | tf_op jit(solution)/shard_map/ppermute | solution.py:29
  216.0 2.4 fusion.35
  218.3 162.0 %all-reduce.2.cloned.1.call-done = f32[768,512]{0,1:T(8,128)} async-done(((f32[768,512]{0,1:T(8,128)}), f32[768,512]{0,1:T(8,128)}) %all-reduce.2.cloned.1.call-update) | async-done | bytes 1572880 | tf_op jit(solution)/shard_map/psum | solution.py:94
  380.3 1.2 constant_dynamic-slice_fusion
  381.5 0.8 copy.10
  382.3 2.0 convolution_bitcast_fusion.3
  384.3 3.5 fusion.8
  (51 shorter events, 0.7 us)
Async XLA Ops:
  6.5 168.2 %copy-start = (bf16[1,1,1152,1152]{3,2,1,0:T(8,128)(2,1)S(1)}, bf16[1,1,1152,1152]{3,2,1,0:T(8,128)(2,1)}, u32[]{:S(2)}) copy-start(bf16[1,1,1152,1152]{3,2,1,0:T(8,128)(2,1)} %param.7) | copy-start | bytes 7962628
  6.5 157.4 %all-gather.2.cloned.1.call-start = ((), (), s32[]{:S(2)}) async-start(), calls=%async_computation | async-start | bytes 1671168 | tf_op jit(solution)/shard_map/all_gather | solution.py:89
  6.5 1.9 copy-start.4
  8.8 14.7 %collective-permute-start = (f32[1,192,704]{2,1,0:T(8,128)S(1)}, f32[1,192,704]{2,1,0:T(8,128)S(1)}, u32[]{:S(2)}, u32[]{:S(2)}) collective-permute-start(f32[1,192,704]{2,1,0:T(8,128)S(1)} %get-tuple-element.23), channel_id=1, source_target_pairs={{0,16},{16,32},{32,48},{48,64},{64,80},{80,96},{96,112},{112,128},... | collective-permute-start | bytes 1622024 | tf_op jit(solution)/shard_map/ppermute | solution.py:18
  10.5 25.8 %collective-permute-start.1 = (f32[1,192,704]{2,1,0:T(8,128)S(1)}, f32[1,192,704]{2,1,0:T(8,128)S(1)}, u32[]{:S(2)}, u32[]{:S(2)}) collective-permute-start(f32[1,192,704]{2,1,0:T(8,128)S(1)} %get-tuple-element.22), channel_id=1, source_target_pairs={{16,0},{32,16},{48,32},{64,48},{80,64},{96,80},{112,96},{128,112},... | collective-permute-start | bytes 1622024 | tf_op jit(solution)/shard_map/ppermute | solution.py:21
  10.8 49.6 %collective-permute-start.2 = (f32[1,192,704]{2,1,0:T(8,128)S(1)}, f32[1,192,704]{2,1,0:T(8,128)S(1)}, u32[]{:S(2)}, u32[]{:S(2)}) collective-permute-start(f32[1,192,704]{2,1,0:T(8,128)S(1)} %get-tuple-element.19), channel_id=1, source_target_pairs={{0,1},{1,2},{2,3},{3,4},{4,5},{5,6},{6,7},{7,8},{8,9},{9,10},{10,1... | collective-permute-start | bytes 1622024 | tf_op jit(solution)/shard_map/ppermute | solution.py:18
  17.0 49.6 %collective-permute-start.3 = (f32[1,192,704]{2,1,0:T(8,128)S(1)}, f32[1,192,704]{2,1,0:T(8,128)S(1)}, u32[]{:S(2)}, u32[]{:S(2)}) collective-permute-start(f32[1,192,704]{2,1,0:T(8,128)S(1)} %get-tuple-element.18), channel_id=1, source_target_pairs={{1,0},{2,1},{3,2},{4,3},{5,4},{6,5},{7,6},{8,7},{9,8},{10,9},{11,1... | collective-permute-start | bytes 1622024 | tf_op jit(solution)/shard_map/ppermute | solution.py:21
  36.4 30.2 %copy-start.12 = (f32[1,192,704]{2,1,0:T(8,128)}, f32[1,192,704]{2,1,0:T(8,128)S(1)}, u32[]{:S(2)}) copy-start(f32[1,192,704]{2,1,0:T(8,128)S(1)} %collective-permute-done.1) | copy-start | bytes 1622020
  60.4 6.2 %copy-start.14 = (f32[1,192,704]{2,1,0:T(8,128)}, f32[1,192,704]{2,1,0:T(8,128)S(1)}, u32[]{:S(2)}) copy-start(f32[1,192,704]{2,1,0:T(8,128)S(1)} %collective-permute-done.2) | copy-start | bytes 1622020
  66.5 0.8 copy-start.16
  67.4 0.9 copy-start.1
  68.7 2.8 copy-start.2
  87.2 2.1 copy-start.9
  87.2 2.3 copy-start.13
  89.3 1.1 copy-start.15
  89.3 1.2 copy-start.17
  90.4 1.7 copy-start.18
  90.8 1.3 copy-start.10
  93.5 286.8 %all-reduce.2.cloned.1.call-start = ((), (), s32[]{:S(2)}) async-start(), calls=%async_computation.1 | async-start | bytes 3145728 | tf_op jit(solution)/shard_map/psum | solution.py:94
  93.8 2.7 copy-start.7
  96.5 1.2 copy-start.3
  103.2 1.5 copy-start.11
  104.3 2.3 copy-start.8
  104.7 1.9 copy-start.5
  186.9 1.4 copy-start.6
  189.4 15.5 %collective-permute-start.4 = (f32[192,512]{1,0:T(8,128)}, f32[192,512]{1,0:T(8,128)}, u32[]{:S(2)}, u32[]{:S(2)}) collective-permute-start(f32[192,512]{1,0:T(8,128)} %get-tuple-element.13), channel_id=1, source_target_pairs={{0,240},{16,0},{32,16},{48,32},{64,48},{80,64},{96,80},{112,96},{1... | collective-permute-start | bytes 1179656 | tf_op jit(solution)/shard_map/ppermute | solution.py:29
  193.4 22.6 %collective-permute-start.5 = (f32[192,512]{1,0:T(8,128)}, f32[192,512]{1,0:T(8,128)}, u32[]{:S(2)}, u32[]{:S(2)}) collective-permute-start(f32[192,512]{1,0:T(8,128)} %get-tuple-element.15), channel_id=1, source_target_pairs={{0,15},{1,0},{2,1},{3,2},{4,3},{5,4},{6,5},{7,6},{8,7},{9,8},{10,9... | collective-permute-start | bytes 1179656 | tf_op jit(solution)/shard_map/ppermute | solution.py:29
  204.8 179.5 %slice-start = ((f32[5,192,192]{2,1,0:T(8,128)}), f32[2,192,192]{2,1,0:T(8,128)S(1)}, s32[]{:S(2)}) async-start(f32[5,192,192]{2,1,0:T(8,128)} %copy-done.8), calls=%async_computation.2 | async-start | bytes 786432 | tf_op jit(solution)/shard_map/slice | solution.py:82
  204.8 179.5 %slice-start.1 = ((f32[5,192,192]{2,1,0:T(8,128)}), f32[1,192,192]{2,1,0:T(8,128)S(1)}, s32[]{:S(2)}) async-start(f32[5,192,192]{2,1,0:T(8,128)} %copy-done.8), calls=%async_computation.3 | async-start | bytes 393216 | tf_op jit(solution)/shard_map/slice | solution.py:82
Sparse Core Ops, SparseCore 0:
  93.6 70.2 all-gather.1
  174.9 205.4 all-reduce.1
where the time goes:
time: 403 us; the launch traced here: 395 us
  waiting for transfers between devices  276 us (68%)
  matrix products  63 us (16%)
  starting transfers between devices  24.1 us (6%)
  between operations  14.1 us (3%)
  local copies, waits for them, and re-layouts  12.7 us (3%)
  other arithmetic  5.35 us (1%)
    psum x1, waiting for transfers between devices, per_device(): summed = lax.psum(incomplete_total, 'narrow')  162 us
    all_gather x1, waiting for transfers between devices, per_device(): lax.all_gather(restricted_residual, 'wide', axis=0, tiled=True)  53.5 us
    ppermute x2, waiting for transfers between devices, extended(): lax.ppermute(lax.slice_in_dim(block, block.shape[dim] - width, None, axis...  30.1 us
    ppermute x2, waiting for transfers between devices, extended(): lax.ppermute(lax.slice_in_dim(block, 0, width, axis=dim), axis, backward)  18.9 us
    dot_general x12, matrix products, newton_schulz(): jnp.einsum('bij,bjk->bik', matrices, approx, precision=exact_arithmetic_m...  16.5 us
    ppermute x2, starting transfers between devices, passed_along(): return lax.ppermute(value, axis, pairs)  15.4 us
    dot_general x12, matrix products, newton_schulz(): jnp.einsum('bij,bjk->bik', approx, product, precision=exact_arithmetic_mode)  14.3 us
    dot_general x4, matrix products, apply_faces(): jnp.einsum('fij,fjr->fir', blocks, fields, precision=exact_arithmetic_mode)  13.4 us
  transfers between devices with their start and end apart: 8, of which 7 were waited for; matrix products, arithmetic and copies ran while one was open for 8% of the time, Pallas kernels for 0%

commit v1 on v0

v1 whole, which is shorter than its diff:
```python
import jax
import jax.numpy as jnp
from jax import lax
from jax.experimental import pallas as pl
from jax.experimental.pallas import tpu as pltpu
from jax.sharding import PartitionSpec as P

NS_STEPS = 12
F = 192
FP = 256
R = 512
CB = 48
HALF = 256
MESH = pl.DeviceIdType.MESH
F32 = jnp.float32
BF16 = jnp.bfloat16


def split(x):
    high = x.astype(BF16)
    return high, (x - high.astype(F32)).astype(BF16)


def mul(a, b):
    return jnp.dot(a, b, preferred_element_type=F32)


def mul3(ah, al, bh, bl):
    return mul(ah, bh) + (mul(ah, bl) + mul(al, bh))


def exact(a, b):
    return jnp.dot(a, b, precision=lax.Precision.HIGHEST, preferred_element_type=F32)


def kernel(
    r_hbm, s_hbm, l_hbm, phi_ref, c_hbm, o_hbm,
    rv, sv, lv, cv, rr, sr, small, small_in, gath,
    part, q1, q2, q3, coarse,
    mh, ml, x, xh, xl, ph, plo, sh, sl,
    bh, bl, loads, wsend, wrecv, comb, ov,
    loc, ss, rs,
):
    w = lax.axis_index("wide")
    n = lax.axis_index("narrow")
    y, zl = w // 4, w % 4
    xx, zh, c = n // 4, (n // 2) % 2, n % 2
    w_up, w_dn = (w + 1) % 16, (w + 15) % 16
    n_up, n_dn = (n + 1) % 16, (n + 15) % 16
    z_peers = [(y * 4 + (zl + d) % 4, n) for d in (1, 2, 3)]
    y_peers = [(((y + d) % 4) * 4 + zl, n) for d in (1, 2, 3)]
    x_peers = [(w, ((xx + d) % 4) * 4 + zh * 2 + c) for d in (1, 2, 3)]
    core_peer = (w, n + 1 - 2 * c)
    far_peer = (w, xx * 4 + (1 - zh) * 2 + c)

    local = [
        pltpu.make_async_copy(s_hbm.at[0, 0], sv, loc.at[0]),
        pltpu.make_async_copy(r_hbm.at[0, 0], rv, loc.at[1]),
        pltpu.make_async_copy(c_hbm, cv, loc.at[2]),
        pltpu.make_async_copy(l_hbm.at[0, 0], lv, loc.at[3]),
    ]
    for copy in local:
        copy.start()

    barrier = pltpu.get_barrier_semaphore()
    greeted = [(w_up, n), (w_dn, n), (w, n_up), (w, n_dn)]
    greeted += z_peers + y_peers + x_peers + [core_peer, far_peer]
    for peer in greeted:
        pl.semaphore_signal(barrier, inc=1, device_id=peer, device_id_type=MESH)
    pl.semaphore_wait(barrier, len(greeted))

    sent = []

    def send(src, dst, peer):
        i = len(sent)
        copy = pltpu.make_async_remote_copy(
            src_ref=src, dst_ref=dst, send_sem=ss.at[i], recv_sem=rs.at[i],
            device_id=peer, device_id_type=MESH,
        )
        copy.start()
        sent.append(copy)
        return copy

    faces_to = {2: (3, (w, n_dn)), 3: (2, (w, n_up)), 0: (1, (w_dn, n)), 1: (0, (w_up, n))}

    s_in = {}
    for f in (2, 3, 0, 1):
        slot, peer = faces_to[f]
        s_in[slot] = send(s_hbm.at[0, 0, f], sr.at[slot], peer)

    phit = [phi_ref[g].T for g in range(3)]
    local[1].wait()
    small[0] = exact(phit[1], rv[2])
    narrow_piece = send(small.at[0], small_in.at[0], (w, n_dn))
    small[1] = exact(phit[0], rv[0])
    wide_piece = send(small.at[1], small_in.at[1], (w_dn, n))
    own0 = exact(phit[0], rv[1])
    own1 = exact(phit[1], rv[3])
    own2 = exact(phit[2], rv[4] + rv[5])
    narrow_piece.wait_recv()
    wide_piece.wait_recv()
    gath[w, 0:16] = own0 + small_in[1]
    gath[w, 16:32] = own1 + small_in[0]
    gath[w, 32:48] = own2
    z_in = [send(gath.at[w], gath.at[w], peer) for peer in z_peers]
    y_in = [send(gath.at[w], gath.at[w], peer) for peer in y_peers]

    r_in = {}
    for f in (2, 3, 0, 1):
        slot, peer = faces_to[f]
        for k in range(2):
            cols = pl.ds(k * HALF, HALF)
            r_in[slot, k] = send(r_hbm.at[0, 0, f, :, cols], rr.at[slot, :, cols], peer)

    local[0].wait()
    sh[...] = jnp.zeros_like(sh)
    sl[...] = jnp.zeros_like(sl)
    mh[...] = jnp.zeros_like(mh)
    ml[...] = jnp.zeros_like(ml)
    x[...] = jnp.zeros_like(x)
    xh[...] = jnp.zeros_like(xh)
    xl[...] = jnp.zeros_like(xl)
    ph[:, F:FP] = jnp.zeros((5, FP - F, FP), BF16)
    plo[:, F:FP] = jnp.zeros((5, FP - F, FP), BF16)
    bh[:, F:FP] = jnp.zeros((6, FP - F, R), BF16)
    bl[:, F:FP] = jnp.zeros((6, FP - F, R), BF16)
    for f in range(6):
        high, low = split(sv[f])
        sh[f, :, 0:F] = high
        sl[f, :, 0:F] = low

    for f in (4, 2, 3, 0, 1):
        if f == 4:
            total = sv[4] + sv[5]
        else:
            s_in[f].wait_recv()
            total = sv[f] + sr[f]
        high, low = split(total)
        mh[f, :, 0:F] = high
        ml[f, :, 0:F] = low
        largest = jnp.max(jnp.sum(jnp.abs(total), axis=1, keepdims=True), axis=0, keepdims=True)
        start = total / (largest * largest)
        x[f, :, 0:F] = start
        high, low = split(start)
        xh[f, 0:F, 0:F] = high
        xl[f, 0:F, 0:F] = low

    def newton(step, carry):
        for f in range(5):
            high, low = split(mul3(mh[f], ml[f], xh[f], xl[f]))
            ph[f, 0:F] = high
            plo[f, 0:F] = low
        for f in range(5):
            new = 2.0 * x[f] - mul3(xh[f, 0:F], xl[f, 0:F], ph[f], plo[f])
            x[f] = new
            high, low = split(new)
            xh[f, 0:F] = high
            xl[f, 0:F] = low
        return carry

    lax.fori_loop(0, 4, newton, 0)
    for copy, d in zip(z_in, (1, 2, 3)):
        copy.wait_recv()
        block = gath.at[y * 4 + (zl + 4 - d) % 4]
        y_in += [send(block, block, peer) for peer in y_peers]
    lax.fori_loop(4, NS_STEPS, newton, 0)

    local[2].wait()
    for copy in y_in:
        copy.wait_recv()
    ch, cl = split(cv[...])
    for k in range(2):
        cols = slice(k * HALF, (k + 1) * HALF)
        gh, gl = split(gath[:, :, cols].reshape(768, HALF))
        value = mul3(ch, cl, gh, gl)
        for j in range(16):
            part[j % 2, j // 2, :, cols] = value[j * CB:(j + 1) * CB]
    pair_in = send(part.at[1 - c], q1, core_peer)
    pair_in.wait_recv()
    for b in range(8):
        part[c, b] = part[c, b] + q1[b]
    x_in = []
    for d in (1, 2, 3):
        first = ((xx + d) % 4) * 2
        x_in.append(send(part.at[c, pl.ds(first, 2)], q2.at[d - 1], x_peers[d - 1]))
    for copy in x_in:
        copy.wait_recv()
    for h in range(2):
        part[c, xx * 2 + h] = part[c, xx * 2 + h] + (q2[0, h] + (q2[1, h] + q2[2, h]))
    far_in = send(part.at[c, xx * 2 + 1 - zh], q3, far_peer)
    far_in.wait_recv()
    coarse[...] = part[c, xx * 2 + zh] + q3[...]

    local[3].wait()
    w_in = {}
    for k in range(2):
        cols = slice(k * HALF, (k + 1) * HALF)
        dcols = pl.ds(k * HALF, HALF)
        for f in (4, 2, 3, 0, 1):
            if f == 4:
                value = rv[4, :, cols] + rv[5, :, cols]
            else:
                r_in[f, k].wait_recv()
                value = rv[f, :, cols] + rr[f, :, cols]
            ah, al = split(value)
            bh[f, 0:F, cols] = ah
            bl[f, 0:F, cols] = al
        for f in range(5):
            high, low = split(mul3(xh[f, 0:F], xl[f, 0:F], bh[f, :, cols], bl[f, :, cols]))
            bh[f, 0:F, cols] = high
            bl[f, 0:F, cols] = low
        for f in range(6):
            s = min(f, 4)
            loads[f * F:(f + 1) * F, cols] = mul3(sh[f], sl[f], bh[s, :, cols], bl[s, :, cols]).astype(BF16)
        for f in (2, 0, 3, 1, 4, 5):
            high, low = split(mul(lv[f * F:(f + 1) * F, :], loads[:, cols]))
            bh[f, 0:F, cols] = high
            bl[f, 0:F, cols] = low
            value = mul3(sh[f], sl[f], bh[f, :, cols], bl[f, :, cols])
            if f == 2:
                wsend[1, :, cols] = value
                w_in[1, k] = send(wsend.at[1, :, dcols], wrecv.at[1, :, dcols], (w, n_dn))
            elif f == 0:
                wsend[0, :, cols] = value
                w_in[0, k] = send(wsend.at[0, :, dcols], wrecv.at[0, :, dcols], (w_dn, n))
            elif f == 5:
                comb[2, :, cols] = comb[2, :, cols] + value
            else:
                comb[f // 2, :, cols] = value

    out = []
    for g in (2, 1, 0):
        low_phi = phi_ref[g]
        for k in range(2):
            cols = slice(k * HALF, (k + 1) * HALF)
            value = comb[g, :, cols]
            if g < 2:
                w_in[g, k].wait_recv()
                value = value + wrecv[g, :, cols]
            high, low = split(value)
            bh[g, 0:F, cols] = high
            bl[g, 0:F, cols] = low
            f = (1, 3, 4)[g]
            ov[g, :, cols] = mul3(
                xh[f, 0:F], xl[f, 0:F], bh[g, :, cols], bl[g, :, cols]
            ) + exact(low_phi, coarse[g * 16:(g + 1) * 16, cols])
        copy = pltpu.make_async_copy(ov.at[g], o_hbm.at[0, 0, g], loc.at[4 + g])
        copy.start()
        out.append(copy)
    for copy in out:
        copy.wait()
    for copy in sent:
        copy.wait_send()


def per_device(residual, face_schur, local_solver, interface_functional_set, coarse_inverse):
    anywhere = pl.BlockSpec(memory_space=pl.ANY)
    vmem = pltpu.VMEM
    return pl.pallas_call(
        kernel,
        out_shape=jax.ShapeDtypeStruct((1, 1, 3, F, R), F32),
        in_specs=[anywhere, anywhere, anywhere, pl.BlockSpec(memory_space=vmem), anywhere],
        out_specs=anywhere,
        scratch_shapes=[
            vmem((6, F, R), F32), vmem((6, F, F), F32), vmem((1152, 1152), BF16), vmem((768, 768), F32),
            vmem((4, F, R), F32), vmem((4, F, F), F32), vmem((2, 16, R), F32), vmem((2, 16, R), F32),
            vmem((16, CB, R), F32),
            vmem((2, 8, CB, R), F32), vmem((8, CB, R), F32), vmem((3, 2, CB, R), F32), vmem((CB, R), F32),
            vmem((CB, R), F32),
            vmem((5, F, FP), BF16), vmem((5, F, FP), BF16), vmem((5, F, FP), F32),
            vmem((5, FP, FP), BF16), vmem((5, FP, FP), BF16), vmem((5, FP, FP), BF16), vmem((5, FP, FP), BF16),
            vmem((6, F, FP), BF16), vmem((6, F, FP), BF16),
            vmem((6, FP, R), BF16), vmem((6, FP, R), BF16), vmem((1152, R), BF16),
            vmem((2, F, R), F32), vmem((2, F, R), F32), vmem((3, F, R), F32), vmem((3, F, R), F32),
            pltpu.SemaphoreType.DMA((7,)), pltpu.SemaphoreType.DMA((48,)), pltpu.SemaphoreType.DMA((48,)),
        ],
        compiler_params=pltpu.CompilerParams(
            collective_id=0, has_side_effects=True, vmem_limit_bytes=56 * 1024 * 1024
        ),
    )(residual, face_schur, local_solver, interface_functional_set, coarse_inverse)


def solution(mesh):
    placed = (
        P("wide", "narrow", None, None, None),
        P("wide", "narrow", None, None, None),
        P("wide", "narrow", None, None),
        P(),
        P("wide", "narrow"),
    )
    return jax.shard_map(
        per_device,
        mesh=mesh,
        in_specs=placed,
        out_specs=P("wide", "narrow", None, None, None),
        check_vma=False,
    )
```

time: 403 us -> 123 us (0.31); the launches traced: 395 us -> 122 us
  waiting for transfers between devices: 276 us -> 0 us
  Pallas kernels: 0 us -> 118 us
  matrix products: 63 us -> 0 us
  starting transfers between devices: 24.1 us -> 0 us
  between operations: 14.1 us -> 0.01 us
  local copies, waits for them, and re-layouts: 12.7 us -> 4.03 us
  other arithmetic: 5.35 us -> 0 us
    psum x1 -> x0, waiting for transfers between devices: 162 us -> none  [per_device(): summed = lax.psum(incomplete_total, 'narrow')]
    pallas_call x0 -> x1, Pallas kernels: none -> 118 us  [per_device(): pl.pallas_call(kernel, out_shape=jax.ShapeDtypeStruct((1, 1, 3, F, R), F3...]
    dot_general x32 -> x0, matrix products: 63 us -> none  [the longest x12 16.5 us: newton_schulz(): jnp.einsum('bij,bjk->bik', matrices, approx, precision=exact_arithmetic_m...]
    ppermute x6 -> x0, waiting for transfers between devices: 60.1 us -> none  [the longest x2 30.1 us: extended(): lax.ppermute(lax.slice_in_dim(block, block.shape[dim] - width, None, axis...]
    all_gather x1 -> x0, waiting for transfers between devices: 53.5 us -> none  [per_device(): lax.all_gather(restricted_residual, 'wide', axis=0, tiled=True)]
    ppermute x6 -> x0, starting transfers between devices: 23.8 us -> none  [the longest x2 15.4 us: passed_along(): return lax.ppermute(value, axis, pairs)]
  transfers between devices with their start and end apart: 8 -> 0, of which waited for: 7 -> 0; matrix products, arithmetic and copies ran while one was open for 8% -> 0% of each run, Pallas kernels for 0% -> 0%
where the time goes in v1:
time: 123 us; the launch traced here: 122 us
  Pallas kernels  118 us (96%)
  local copies, waits for them, and re-layouts  4.03 us (3%)
    pallas_call x1, Pallas kernels, per_device(): pl.pallas_call(kernel, out_shape=jax.ShapeDtypeStruct((1, 1, 3, F, R), F3...  118 us
    unnamed x2, local copies, waits for them, and re-layouts  4.03 us

profile of v1, /device:TPU:65, one launch (start us, length us, event | category | flops | bytes accessed | tf_op | source)
XLA Modules:
  0.0 122.3 jit_solution(2029145551987850860)
XLA Ops:
  0.0 1.7 %copy.6.phi_ref = f32[3,192,16]{2,1,0:T(8,128)} copy(f32[3,192,16]{1,2,0:T(8,128)} %param.8) | data formatting | bytes 73728 | tf_op args[3]
  1.7 118.3 %shard_map.55 = f32[1,1,3,192,512]{4,3,2,1,0:T(8,128)} custom-call(f32[1,1,6,192,512]{4,3,2,1,0:T(8,128)} %r_hbm.1, f32[1,1,6,192,192]{4,3,2,1,0:T(8,128)} %s_hbm.1, bf16[1,1,1152,1152]{3,2,1,0:T(8,128)(2,1)} %l_hbm.1, f32[3,192,16]{2,1,0:T(8,128)} %copy.6.phi_ref, f32[768,768]{1,0:T(8,128)} %c_hbm.1), custom_call_target="tpu_custom_call" | custom-call | tf_op jit(solution)/shard_map/pallas_call | solution.py:259
  120.0 2.4 %copy.8 = f32[1,1,3,192,512]{4,3,2,1,0:T(8,128)} copy(f32[1,1,3,192,512]{4,3,2,1,0:T(8,128)} %shard_map.55) | data formatting | bytes 2359296

commit v2 on v1

--- a/solution.py
+++ b/solution.py
@@ -11,6 +11,10 @@
 R = 512
 CB = 48
 HALF = 256
+CHUNKS = ((0, 128), (128, 128), (256, 128), (384, 128))
+EARLY = ("n0", "w0")
+DURING = ((0, "n1"), (0, "w1"), (3, "fw"), (4, "n2"), (4, "w2"), (7, "n3"), (7, "w3"))
+AFTER = ("l0", "cp", "l1", "cf", "l2", "l3", "ce")
 MESH = pl.DeviceIdType.MESH
 F32 = jnp.float32
 BF16 = jnp.bfloat16
@@ -35,7 +39,7 @@
 
 def kernel(
     r_hbm, s_hbm, l_hbm, phi_ref, c_hbm, o_hbm,
-    rv, sv, lv, cv, rr, sr, small, small_in, gath,
+    rv, sv, lv, cv, rr, sr, spk, spk_in, small, small_in, gath,
     part, q1, q2, q3, coarse,
     mh, ml, x, xh, xl, ph, plo, sh, sl,
     bh, bl, loads, wsend, wrecv, comb, ov,
@@ -59,14 +63,23 @@
         pltpu.make_async_copy(c_hbm, cv, loc.at[2]),
         pltpu.make_async_copy(l_hbm.at[0, 0], lv, loc.at[3]),
     ]
-    for copy in local:
-        copy.start()
+    local[0].start()
+    local[1].start()
 
     barrier = pltpu.get_barrier_semaphore()
     greeted = [(w_up, n), (w_dn, n), (w, n_up), (w, n_dn)]
     greeted += z_peers + y_peers + x_peers + [core_peer, far_peer]
     for peer in greeted:
         pl.semaphore_signal(barrier, inc=1, device_id=peer, device_id_type=MESH)
+
+    left = lax.broadcasted_iota(jnp.int32, (64, 128), 1) < 64
+    local[0].wait()
+    for f in range(4):
+        top, middle, bottom = (sv[f, 64 * i:64 * i + 64, 0:128] for i in range(3))
+        spk[f, 0:64] = jnp.where(left, top, middle)
+        spk[f, 64:128] = bottom
+        spk[f, 64:128, 0:64] = sv[f, 128:192, 128:192]
+        spk[f, 128:192] = jnp.where(left, bottom, top)
     pl.semaphore_wait(barrier, len(greeted))
 
     sent = []
@@ -86,7 +99,9 @@
     s_in = {}
     for f in (2, 3, 0, 1):
         slot, peer = faces_to[f]
-        s_in[slot] = send(s_hbm.at[0, 0, f], sr.at[slot], peer)
+        s_in[slot] = send(spk.at[f], spk_in.at[slot], peer)
+    local[2].start()
+    local[3].start()
 
     phit = [phi_ref[g].T for g in range(3)]
     local[1].wait()
@@ -106,13 +121,27 @@
     y_in = [send(gath.at[w], gath.at[w], peer) for peer in y_peers]
 
     r_in = {}
-    for f in (2, 3, 0, 1):
-        slot, peer = faces_to[f]
-        for k in range(2):
-            cols = pl.ds(k * HALF, HALF)
+
+    def send_loads(faces, k):
+        cols = pl.ds(*CHUNKS[k])
+        for f in faces:
+            slot, peer = faces_to[f]
             r_in[slot, k] = send(r_hbm.at[0, 0, f, :, cols], rr.at[slot, :, cols], peer)
 
-    local[0].wait()
+    def forward():
+        for copy, d in zip(z_in, (1, 2, 3)):
+            copy.wait_recv()
+            block = gath.at[y * 4 + (zl + 4 - d) % 4]
+            for peer in y_peers:
+                y_in.append(send(block, block, peer))
+
+    actions = {"fw": forward}
+    for k in range(len(CHUNKS)):
+        actions[f"n{k}"] = lambda k=k: send_loads((2, 3), k)
+        actions[f"w{k}"] = lambda k=k: send_loads((0, 1), k)
+    for name in EARLY:
+        actions[name]()
+
     sh[...] = jnp.zeros_like(sh)
     sl[...] = jnp.zeros_like(sl)
     mh[...] = jnp.zeros_like(mh)
@@ -134,6 +163,15 @@
             total = sv[4] + sv[5]
         else:
             s_in[f].wait_recv()
+            first, second, third = (spk_in[f, 64 * i:64 * i + 64] for i in range(3))
+            second_t, third_t = second.T, third.T
+            sr[f, 0:64, 0:128] = jnp.where(left, first, third)
+            sr[f, 64:128, 0:128] = first
+            sr[f, 64:128, 0:64] = third_t[64:128]
+            sr[f, 128:192, 0:128] = jnp.where(left, third, second)
+            sr[f, 0:64, 128:192] = third_t[0:64]
+            sr[f, 64:128, 128:192] = second_t[64:128]
+            sr[f, 128:192, 128:192] = second[:, 0:64]
             total = sv[f] + sr[f]
         high, low = split(total)
         mh[f, :, 0:F] = high
@@ -158,44 +196,21 @@
             xl[f, 0:F] = low
         return carry
 
-    lax.fori_loop(0, 4, newton, 0)
-    for copy, d in zip(z_in, (1, 2, 3)):
-        copy.wait_recv()
-        block = gath.at[y * 4 + (zl + 4 - d) % 4]
-        y_in += [send(block, block, peer) for peer in y_peers]
-    lax.fori_loop(4, NS_STEPS, newton, 0)
-
-    local[2].wait()
-    for copy in y_in:
-        copy.wait_recv()
-    ch, cl = split(cv[...])
-    for k in range(2):
-        cols = slice(k * HALF, (k + 1) * HALF)
-        gh, gl = split(gath[:, :, cols].reshape(768, HALF))
-        value = mul3(ch, cl, gh, gl)
-        for j in range(16):
-            part[j % 2, j // 2, :, cols] = value[j * CB:(j + 1) * CB]
-    pair_in = send(part.at[1 - c], q1, core_peer)
-    pair_in.wait_recv()
-    for b in range(8):
-        part[c, b] = part[c, b] + q1[b]
-    x_in = []
-    for d in (1, 2, 3):
-        first = ((xx + d) % 4) * 2
-        x_in.append(send(part.at[c, pl.ds(first, 2)], q2.at[d - 1], x_peers[d - 1]))
-    for copy in x_in:
-        copy.wait_recv()
-    for h in range(2):
-        part[c, xx * 2 + h] = part[c, xx * 2 + h] + (q2[0, h] + (q2[1, h] + q2[2, h]))
-    far_in = send(part.at[c, xx * 2 + 1 - zh], q3, far_peer)
-    far_in.wait_recv()
-    coarse[...] = part[c, xx * 2 + zh] + q3[...]
-
-    local[3].wait()
+    done = 0
+    for step, name in DURING:
+        if step > done:
+            lax.fori_loop(done, step, newton, 0)
+            done = step
+        actions[name]()
+    if done < NS_STEPS:
+        lax.fori_loop(done, NS_STEPS, newton, 0)
+
     w_in = {}
-    for k in range(2):
-        cols = slice(k * HALF, (k + 1) * HALF)
-        dcols = pl.ds(k * HALF, HALF)
+
+    def local_part(k):
+        begin, width = CHUNKS[k]
+        cols = slice(begin, begin + width)
+        dcols = pl.ds(begin, width)
         for f in (4, 2, 3, 0, 1):
             if f == 4:
                 value = rv[4, :, cols] + rv[5, :, cols]
@@ -205,13 +220,13 @@
             ah, al = split(value)
             bh[f, 0:F, cols] = ah
             bl[f, 0:F, cols] = al
-        for f in range(5):
             high, low = split(mul3(xh[f, 0:F], xl[f, 0:F], bh[f, :, cols], bl[f, :, cols]))
             bh[f, 0:F, cols] = high
             bl[f, 0:F, cols] = low
-        for f in range(6):
-            s = min(f, 4)
-            loads[f * F:(f + 1) * F, cols] = mul3(sh[f], sl[f], bh[s, :, cols], bl[s, :, cols]).astype(BF16)
+            for g in ((4, 5) if f == 4 else (f,)):
+                loads[g * F:(g + 1) * F, cols] = mul3(
+                    sh[g], sl[g], bh[f, :, cols], bl[f, :, cols]
+                ).astype(BF16)
         for f in (2, 0, 3, 1, 4, 5):
             high, low = split(mul(lv[f * F:(f + 1) * F, :], loads[:, cols]))
             bh[f, 0:F, cols] = high
@@ -228,25 +243,77 @@
             else:
                 comb[f // 2, :, cols] = value
 
-    out = []
-    for g in (2, 1, 0):
-        low_phi = phi_ref[g]
+    x_in = []
+
+    def coarse_product():
+        for copy in y_in:
+            copy.wait_recv()
+        ch, cl = split(cv[...])
         for k in range(2):
             cols = slice(k * HALF, (k + 1) * HALF)
-            value = comb[g, :, cols]
-            if g < 2:
-                w_in[g, k].wait_recv()
-                value = value + wrecv[g, :, cols]
-            high, low = split(value)
-            bh[g, 0:F, cols] = high
-            bl[g, 0:F, cols] = low
-            f = (1, 3, 4)[g]
-            ov[g, :, cols] = mul3(
-                xh[f, 0:F], xl[f, 0:F], bh[g, :, cols], bl[g, :, cols]
-            ) + exact(low_phi, coarse[g * 16:(g + 1) * 16, cols])
-        copy = pltpu.make_async_copy(ov.at[g], o_hbm.at[0, 0, g], loc.at[4 + g])
+            gh, gl = split(gath[:, :, cols].reshape(768, HALF))
+            value = mul3(ch, cl, gh, gl)
+            for j in range(16):
+                part[j % 2, j // 2, :, cols] = value[j * CB:(j + 1) * CB]
+        pair_in = send(part.at[1 - c], q1, core_peer)
+        pair_in.wait_recv()
+        for b in range(8):
+            part[c, b] = part[c, b] + q1[b]
+        for d in (1, 2, 3):
+            first = ((xx + d) % 4) * 2
+            x_in.append(send(part.at[c, pl.ds(first, 2)], q2.at[d - 1], x_peers[d - 1]))
+
+    far = []
+
+    def coarse_far():
+        for copy in x_in:
+            copy.wait_recv()
+        for h in range(2):
+            part[c, xx * 2 + h] = part[c, xx * 2 + h] + (q2[0, h] + (q2[1, h] + q2[2, h]))
+        far.append(send(part.at[c, xx * 2 + 1 - zh], q3, far_peer))
+
+    def coarse_end():
+        far[0].wait_recv()
+        coarse[...] = part[c, xx * 2 + zh] + q3[...]
+        for g in range(3):
+            ov[g] = exact(phi_ref[g], coarse[g * 16:(g + 1) * 16])
+
+    out = []
+
+    def finish(g, k):
+        begin, width = CHUNKS[k]
+        cols = slice(begin, begin + width)
+        dcols = pl.ds(begin, width)
+        value = comb[g, :, cols]
+        if g < 2:
+            w_in[g, k].wait_recv()
+            value = value + wrecv[g, :, cols]
+        high, low = split(value)
+        bh[g, 0:F, cols] = high
+        bl[g, 0:F, cols] = low
+        f = (1, 3, 4)[g]
+        ov[g, :, cols] = ov[g, :, cols] + mul3(
+            xh[f, 0:F], xl[f, 0:F], bh[g, :, cols], bl[g, :, cols]
+        )
+        copy = pltpu.make_async_copy(
+            ov.at[g, :, dcols], o_hbm.at[0, 0, g, :, dcols], loc.at[4 + len(out)]
+        )
         copy.start()
         out.append(copy)
+
+    local[2].wait()
+    local[3].wait()
+    steps = {"cp": coarse_product, "cf": coarse_far, "ce": coarse_end}
+    for k in range(len(CHUNKS)):
+        steps[f"l{k}"] = lambda k=k: local_part(k)
+    for name in AFTER:
+        steps[name]()
+
+    for k in range(len(CHUNKS)):
+        finish(2, k)
+    for k in range(len(CHUNKS)):
+        finish(1, k)
+        finish(0, k)
     for copy in out:
         copy.wait()
     for copy in sent:
@@ -263,7 +330,7 @@
         out_specs=anywhere,
         scratch_shapes=[
             vmem((6, F, R), F32), vmem((6, F, F), F32), vmem((1152, 1152), BF16), vmem((768, 768), F32),
-            vmem((4, F, R), F32), vmem((4, F, F), F32), vmem((2, 16, R), F32), vmem((2, 16, R), F32),
+            vmem((4, F, R), F32), vmem((4, F, F), F32), vmem((4, F, 128), F32), vmem((4, F, 128), F32), vmem((2, 16, R), F32), vmem((2, 16, R), F32),
             vmem((16, CB, R), F32),
             vmem((2, 8, CB, R), F32), vmem((8, CB, R), F32), vmem((3, 2, CB, R), F32), vmem((CB, R), F32),
             vmem((CB, R), F32),
@@ -272,7 +339,7 @@
             vmem((6, F, FP), BF16), vmem((6, F, FP), BF16),
             vmem((6, FP, R), BF16), vmem((6, FP, R), BF16), vmem((1152, R), BF16),
             vmem((2, F, R), F32), vmem((2, F, R), F32), vmem((3, F, R), F32), vmem((3, F, R), F32),
-            pltpu.SemaphoreType.DMA((7,)), pltpu.SemaphoreType.DMA((48,)), pltpu.SemaphoreType.DMA((48,)),
+            pltpu.SemaphoreType.DMA((16,)), pltpu.SemaphoreType.DMA((64,)), pltpu.SemaphoreType.DMA((64,)),
         ],
         compiler_params=pltpu.CompilerParams(
             collective_id=0, has_side_effects=True, vmem_limit_bytes=56 * 1024 * 1024

time: 123 us -> 97.3 us (0.79)
  the two profiles are of different devices: /device:TPU:65 before, /device:TPU:84 now
where the time goes in v2:
time: 97.3 us; the launch traced here: 97.1 us
  Pallas kernels  93 us (96%)
  local copies, waits for them, and re-layouts  4.03 us (4%)
    pallas_call x1, Pallas kernels, per_device(): pl.pallas_call(kernel, out_shape=jax.ShapeDtypeStruct((1, 1, 3, F, R), F3...  93 us
    unnamed x2, local copies, waits for them, and re-layouts  4.03 us

profile of v2, /device:TPU:84, one launch (start us, length us, event | category | flops | bytes accessed | tf_op | source)
XLA Modules:
  0.0 97.1 jit_solution(2858326690479912987)
XLA Ops:
  0.0 1.7 %copy.6.phi_ref = f32[3,192,16]{2,1,0:T(8,128)} copy(f32[3,192,16]{1,2,0:T(8,128)} %param.8) | data formatting | bytes 73728 | tf_op args[3]
  1.7 93.0 %shard_map.55 = f32[1,1,3,192,512]{4,3,2,1,0:T(8,128)} custom-call(f32[1,1,6,192,512]{4,3,2,1,0:T(8,128)} %r_hbm.1, f32[1,1,6,192,192]{4,3,2,1,0:T(8,128)} %s_hbm.1, bf16[1,1,1152,1152]{3,2,1,0:T(8,128)(2,1)} %l_hbm.1, f32[3,192,16]{2,1,0:T(8,128)} %copy.6.phi_ref, f32[768,768]{1,0:T(8,128)} %c_hbm.1), custom_call_target="tpu_custom_call" | custom-call | tf_op jit(solution)/shard_map/pallas_call | solution.py:326
  94.7 2.4 %copy.8 = f32[1,1,3,192,512]{4,3,2,1,0:T(8,128)} copy(f32[1,1,3,192,512]{4,3,2,1,0:T(8,128)} %shard_map.55) | data formatting | bytes 2359296

commit v3 on v2

v3 whole, which is shorter than its diff:
```python
import jax
import jax.numpy as jnp
from jax import lax
from jax.experimental import pallas as pl
from jax.experimental.pallas import tpu as pltpu
from jax.sharding import PartitionSpec as P

NS_STEPS = 12
F = 192
FP = 256
R = 512
CB = 48
HALF = 256
CHUNKS = ((0, 128), (128, 256), (384, 128))
EARLY = ("n0", "w0")
DURING = ((0, "n1"), (0, "w1"), (0, "n2"), (0, "w2"), (4, "fw"))
AFTER = ("s0", "s1", "s2", "l0", "cp", "cx", "l1", "cf", "l2", "ce")
MESH = pl.DeviceIdType.MESH
F32 = jnp.float32
BF16 = jnp.bfloat16


def split(x):
    high = x.astype(BF16)
    return high, (x - high.astype(F32)).astype(BF16)


def mul(a, b):
    return jnp.dot(a, b, preferred_element_type=F32)


def mul3(ah, al, bh, bl):
    return mul(ah, bh) + (mul(ah, bl) + mul(al, bh))


def thin(ah, al, b):
    bh, bl = split(b)
    both = mul(jnp.concatenate([ah, al], axis=0), bh)
    rows = ah.shape[0]
    return both[:rows] + (both[rows:] + mul(ah, bl))


def exact(a, b):
    return jnp.dot(a, b, precision=lax.Precision.HIGHEST, preferred_element_type=F32)


def kernel(
    r_hbm, s_hbm, l_hbm, phi_ref, c_hbm, o_hbm,
    rv, sv, lv, cv, rr, sr, spk, spk_in, small, small_in, gath,
    part, q1, q2, q3, coarse,
    mh, ml, x, xh, xl, ph, plo, sh, sl,
    bh, bl, loads, ssend, srecv, wsend, wrecv, comb, ov,
    loc, ss, rs,
):
    w = lax.axis_index("wide")
    n = lax.axis_index("narrow")
    y, zl = w // 4, w % 4
    xx, zh, c = n // 4, (n // 2) % 2, n % 2
    w_up, w_dn = (w + 1) % 16, (w + 15) % 16
    n_up, n_dn = (n + 1) % 16, (n + 15) % 16
    z_peers = [(y * 4 + (zl + d) % 4, n) for d in (1, 2, 3)]
    y_peers = [(((y + d) % 4) * 4 + zl, n) for d in (1, 2, 3)]
    x_peers = [(w, ((xx + d) % 4) * 4 + zh * 2 + c) for d in (1, 2, 3)]
    core_peer = (w, n + 1 - 2 * c)
    far_peer = (w, xx * 4 + (1 - zh) * 2 + c)

    local = [
        pltpu.make_async_copy(s_hbm.at[0, 0], sv, loc.at[0]),
        pltpu.make_async_copy(r_hbm.at[0, 0], rv, loc.at[1]),
        pltpu.make_async_copy(c_hbm, cv, loc.at[2]),
        pltpu.make_async_copy(l_hbm.at[0, 0], lv, loc.at[3]),
    ]
    local[0].start()
    local[1].start()

    barrier = pltpu.get_barrier_semaphore()
    greeted = [(w_up, n), (w_dn, n), (w, n_up), (w, n_dn)]
    greeted += z_peers + y_peers + x_peers + [core_peer, far_peer]
    for peer in greeted:
        pl.semaphore_signal(barrier, inc=1, device_id=peer, device_id_type=MESH)

    left = lax.broadcasted_iota(jnp.int32, (64, 128), 1) < 64
    local[0].wait()
    for g in range(2):
        top, middle, bottom = (sv[2 * g, 64 * i:64 * i + 64, 0:128] for i in range(3))
        spk[g, 0:64] = jnp.where(left, top, middle)
        spk[g, 64:128] = bottom
        spk[g, 64:128, 0:64] = sv[2 * g, 128:192, 128:192]
        spk[g, 128:192] = jnp.where(left, bottom, top)
    pl.semaphore_wait(barrier, len(greeted))

    sent = []

    def send(src, dst, peer):
        i = len(sent)
        copy = pltpu.make_async_remote_copy(
            src_ref=src, dst_ref=dst, send_sem=ss.at[i], recv_sem=rs.at[i],
            device_id=peer, device_id_type=MESH,
        )
        copy.start()
        sent.append(copy)
        return copy

    lower = ((w_dn, n), (w, n_dn))
    upper = ((w_up, n), (w, n_up))
    s_in = {g: send(spk.at[g], spk_in.at[g], lower[g]) for g in (1, 0)}
    local[2].start()
    local[3].start()

    phit = [split(phi_ref[g]) for g in range(3)]
    local[1].wait()
    small[0] = thin(*phit[1], rv[2])
    narrow_piece = send(small.at[0], small_in.at[0], (w, n_dn))
    small[1] = thin(*phit[0], rv[0])
    wide_piece = send(small.at[1], small_in.at[1], (w_dn, n))
    own0 = thin(*phit[0], rv[1])
    own1 = thin(*phit[1], rv[3])
    own2 = thin(*phit[2], rv[4] + rv[5])
    narrow_piece.wait_recv()
    wide_piece.wait_recv()
    gath[w, 0:16] = own0 + small_in[1]
    gath[w, 16:32] = own1 + small_in[0]
    gath[w, 32:48] = own2
    z_in = [send(gath.at[w], gath.at[w], peer) for peer in z_peers]
    y_in = [send(gath.at[w], gath.at[w], peer) for peer in y_peers]

    r_in = {}

    def send_loads(g, k):
        cols = pl.ds(*CHUNKS[k])
        r_in[g, k] = send(r_hbm.at[0, 0, 2 * g, :, cols], rr.at[g, :, cols], lower[g])

    def forward():
        for copy, d in zip(z_in, (1, 2, 3)):
            copy.wait_recv()
            block = gath.at[y * 4 + (zl + 4 - d) % 4]
            for peer in y_peers:
                y_in.append(send(block, block, peer))

    actions = {"fw": forward}
    for k in range(len(CHUNKS)):
        actions[f"n{k}"] = lambda k=k: send_loads(1, k)
        actions[f"w{k}"] = lambda k=k: send_loads(0, k)
    for name in EARLY:
        actions[name]()

    sh[...] = jnp.zeros_like(sh)
    sl[...] = jnp.zeros_like(sl)
    mh[...] = jnp.zeros_like(mh)
    ml[...] = jnp.zeros_like(ml)
    x[...] = jnp.zeros_like(x)
    xh[...] = jnp.zeros_like(xh)
    xl[...] = jnp.zeros_like(xl)
    ph[:, F:FP] = jnp.zeros((3, FP - F, FP), BF16)
    plo[:, F:FP] = jnp.zeros((3, FP - F, FP), BF16)
    bh[:, F:FP] = jnp.zeros((6, FP - F, R), BF16)
    bl[:, F:FP] = jnp.zeros((6, FP - F, R), BF16)
    for f in range(6):
        high, low = split(sv[f])
        sh[f, :, 0:F] = high
        sl[f, :, 0:F] = low

    for g in (2, 1, 0):
        if g == 2:
            total = sv[4] + sv[5]
        else:
            s_in[g].wait_recv()
            first, second, third = (spk_in[g, 64 * i:64 * i + 64] for i in range(3))
            second_t, third_t = second.T, third.T
            sr[g, 0:64, 0:128] = jnp.where(left, first, third)
            sr[g, 64:128, 0:128] = first
            sr[g, 64:128, 0:64] = third_t[64:128]
            sr[g, 128:192, 0:128] = jnp.where(left, third, second)
            sr[g, 0:64, 128:192] = third_t[0:64]
            sr[g, 64:128, 128:192] = second_t[64:128]
            sr[g, 128:192, 128:192] = second[:, 0:64]
            total = sv[2 * g + 1] + sr[g]
        high, low = split(total)
        mh[g, :, 0:F] = high
        ml[g, :, 0:F] = low
        largest = jnp.max(jnp.sum(jnp.abs(total), axis=1, keepdims=True), axis=0, keepdims=True)
        start = total / (largest * largest)
        x[g, :, 0:F] = start
        high, low = split(start)
        xh[g, 0:F, 0:F] = high
        xl[g, 0:F, 0:F] = low

    def newton(step, carry):
        for g in range(3):
            high, low = split(mul3(mh[g], ml[g], xh[g], xl[g]))
            ph[g, 0:F] = high
            plo[g, 0:F] = low
        for g in range(3):
            new = 2.0 * x[g] - mul3(xh[g, 0:F], xl[g, 0:F], ph[g], plo[g])
            x[g] = new
            high, low = split(new)
            xh[g, 0:F] = high
            xl[g, 0:F] = low
        return carry

    done = 0
    for step, name in DURING:
        if step > done:
            lax.fori_loop(done, step, newton, 0)
            done = step
        actions[name]()
    if done < NS_STEPS:
        lax.fori_loop(done, NS_STEPS, newton, 0)

    w_in = {}

    y_scaled = {}

    def face_loads(f, slot, cols):
        loads[f * F:(f + 1) * F, cols] = mul3(
            sh[f], sl[f], bh[slot, :, cols], bl[slot, :, cols]
        ).astype(BF16)

    def scaled_part(k):
        begin, width = CHUNKS[k]
        cols = slice(begin, begin + width)
        dcols = pl.ds(begin, width)
        for g in (1, 0, 2):
            if g == 2:
                value = rv[4, :, cols] + rv[5, :, cols]
            else:
                r_in[g, k].wait_recv()
                value = rv[2 * g + 1, :, cols] + rr[g, :, cols]
            f = (1, 3, 4)[g]
            high, low = split(value)
            bh[f, 0:F, cols] = high
            bl[f, 0:F, cols] = low
            value = mul3(xh[g, 0:F], xl[g, 0:F], bh[f, :, cols], bl[f, :, cols])
            if g < 2:
                ssend[g, :, cols] = value
                y_scaled[g, k] = send(ssend.at[g, :, dcols], srecv.at[g, :, dcols], upper[g])
            high, low = split(value)
            bh[f, 0:F, cols] = high
            bl[f, 0:F, cols] = low
        for f in (1, 3, 4, 5):
            face_loads(f, min(f, 4), cols)

    def local_part(k):
        begin, width = CHUNKS[k]
        cols = slice(begin, begin + width)
        dcols = pl.ds(begin, width)
        for g in (0, 1):
            y_scaled[g, k].wait_recv()
            high, low = split(srecv[g, :, cols])
            bh[2 * g, 0:F, cols] = high
            bl[2 * g, 0:F, cols] = low
            face_loads(2 * g, 2 * g, cols)
        for f in (2, 0, 3, 1, 4, 5):
            high, low = split(mul(lv[f * F:(f + 1) * F, :], loads[:, cols]))
            bh[f, 0:F, cols] = high
            bl[f, 0:F, cols] = low
            value = mul3(sh[f], sl[f], bh[f, :, cols], bl[f, :, cols])
            if f == 2:
                wsend[1, :, cols] = value
                w_in[1, k] = send(wsend.at[1, :, dcols], wrecv.at[1, :, dcols], (w, n_dn))
            elif f == 0:
                wsend[0, :, cols] = value
                w_in[0, k] = send(wsend.at[0, :, dcols], wrecv.at[0, :, dcols], (w_dn, n))
            elif f == 5:
                comb[2, :, cols] = comb[2, :, cols] + value
            else:
                comb[f // 2, :, cols] = value

    x_in = []
    pair_in = []

    def coarse_product():
        for copy in y_in:
            copy.wait_recv()
        ch, cl = split(cv[...])
        for k in range(2):
            cols = slice(k * HALF, (k + 1) * HALF)
            gh, gl = split(gath[:, :, cols].reshape(768, HALF))
            value = mul3(ch, cl, gh, gl)
            for j in range(16):
                part[j % 2, j // 2, :, cols] = value[j * CB:(j + 1) * CB]
            dcols = pl.ds(k * HALF, HALF)
            pair_in.append(send(part.at[1 - c, :, :, dcols], q1.at[:, :, dcols], core_peer))

    def coarse_pair():
        for k in range(2):
            cols = slice(k * HALF, (k + 1) * HALF)
            dcols = pl.ds(k * HALF, HALF)
            pair_in[k].wait_recv()
            for b in range(8):
                part[c, b, :, cols] = part[c, b, :, cols] + q1[b, :, cols]
            for d in (1, 2, 3):
                first = ((xx + d) % 4) * 2
                x_in.append(send(
                    part.at[c, pl.ds(first, 2), :, dcols], q2.at[d - 1, :, :, dcols], x_peers[d - 1]
                ))

    far = []

    def coarse_far():
        for k in range(2):
            cols = slice(k * HALF, (k + 1) * HALF)
            dcols = pl.ds(k * HALF, HALF)
            for copy in x_in[3 * k:3 * k + 3]:
                copy.wait_recv()
            for h in range(2):
                part[c, xx * 2 + h, :, cols] = part[c, xx * 2 + h, :, cols] + (
                    q2[0, h, :, cols] + (q2[1, h, :, cols] + q2[2, h, :, cols])
                )
            far.append(send(part.at[c, xx * 2 + 1 - zh, :, dcols], q3.at[:, dcols], far_peer))

    def coarse_end():
        for copy in far:
            copy.wait_recv()
        coarse[...] = part[c, xx * 2 + zh] + q3[...]
        for g in range(3):
            ov[g] = exact(phi_ref[g].T, coarse[g * 16:(g + 1) * 16])

    out = []

    def finish(g, k):
        begin, width = CHUNKS[k]
        cols = slice(begin, begin + width)
        dcols = pl.ds(begin, width)
        value = comb[g, :, cols]
        if g < 2:
            w_in[g, k].wait_recv()
            value = value + wrecv[g, :, cols]
        high, low = split(value)
        bh[g, 0:F, cols] = high
        bl[g, 0:F, cols] = low
        ov[g, :, cols] = ov[g, :, cols] + mul3(
            xh[g, 0:F], xl[g, 0:F], bh[g, :, cols], bl[g, :, cols]
        )
        copy = pltpu.make_async_copy(
            ov.at[g, :, dcols], o_hbm.at[0, 0, g, :, dcols], loc.at[4 + len(out)]
        )
        copy.start()
        out.append(copy)

    local[2].wait()
    local[3].wait()
    steps = {"cp": coarse_product, "cx": coarse_pair, "cf": coarse_far, "ce": coarse_end}
    for k in range(len(CHUNKS)):
        steps[f"s{k}"] = lambda k=k: scaled_part(k)
        steps[f"l{k}"] = lambda k=k: local_part(k)
    for name in AFTER:
        steps[name]()

    for k in range(len(CHUNKS)):
        finish(2, k)
    for k in range(len(CHUNKS)):
        finish(1, k)
        finish(0, k)
    for copy in out:
        copy.wait()
    for copy in sent:
        copy.wait_send()


def per_device(residual, face_schur, local_solver, interface_functional_set, coarse_inverse):
    anywhere = pl.BlockSpec(memory_space=pl.ANY)
    vmem = pltpu.VMEM
    return pl.pallas_call(
        kernel,
        out_shape=jax.ShapeDtypeStruct((1, 1, 3, F, R), F32),
        in_specs=[anywhere, anywhere, anywhere, pl.BlockSpec(memory_space=vmem), anywhere],
        out_specs=anywhere,
        scratch_shapes=[
            vmem((6, F, R), F32), vmem((6, F, F), F32), vmem((1152, 1152), BF16), vmem((768, 768), F32),
            vmem((2, F, R), F32), vmem((2, F, F), F32), vmem((2, F, 128), F32), vmem((2, F, 128), F32), vmem((2, 16, R), F32), vmem((2, 16, R), F32),
            vmem((16, CB, R), F32),
            vmem((2, 8, CB, R), F32), vmem((8, CB, R), F32), vmem((3, 2, CB, R), F32), vmem((CB, R), F32),
            vmem((CB, R), F32),
            vmem((3, F, FP), BF16), vmem((3, F, FP), BF16), vmem((3, F, FP), F32),
            vmem((3, FP, FP), BF16), vmem((3, FP, FP), BF16), vmem((3, FP, FP), BF16), vmem((3, FP, FP), BF16),
            vmem((6, F, FP), BF16), vmem((6, F, FP), BF16),
            vmem((6, FP, R), BF16), vmem((6, FP, R), BF16), vmem((1152, R), BF16),
            vmem((2, F, R), F32), vmem((2, F, R), F32), vmem((2, F, R), F32), vmem((2, F, R), F32), vmem((3, F, R), F32), vmem((3, F, R), F32),
            pltpu.SemaphoreType.DMA((16,)), pltpu.SemaphoreType.DMA((64,)), pltpu.SemaphoreType.DMA((64,)),
        ],
        compiler_params=pltpu.CompilerParams(
            collective_id=0, has_side_effects=True, vmem_limit_bytes=56 * 1024 * 1024
        ),
    )(residual, face_schur, local_solver, jnp.swapaxes(interface_functional_set, 1, 2), coarse_inverse)


def solution(mesh):
    placed = (
        P("wide", "narrow", None, None, None),
        P("wide", "narrow", None, None, None),
        P("wide", "narrow", None, None),
        P(),
        P("wide", "narrow"),
    )
    return jax.shard_map(
        per_device,
        mesh=mesh,
        in_specs=placed,
        out_specs=P("wide", "narrow", None, None, None),
        check_vma=False,
    )
```

time: 97.3 us -> 93.9 us (0.965)
  the two profiles are of different devices: /device:TPU:84 before, /device:TPU:29 now
where the time goes in v3:
time: 93.9 us; the launch traced here: 93.8 us
  Pallas kernels  91.4 us (97%)
  local copies, waits for them, and re-layouts  2.36 us (3%)
    pallas_call x1, Pallas kernels, per_device(): pl.pallas_call(kernel, out_shape=jax.ShapeDtypeStruct((1, 1, 3, F, R), F3...  91.4 us
    unnamed x1, local copies, waits for them, and re-layouts  2.36 us

profile of v3, /device:TPU:29, one launch (start us, length us, event | category | flops | bytes accessed | tf_op | source)
XLA Modules:
  0.0 93.8 jit_solution(15199204503939408487)
XLA Ops:
  0.0 91.4 %shard_map.55 = f32[1,1,3,192,512]{4,3,2,1,0:T(8,128)} custom-call(f32[1,1,6,192,512]{4,3,2,1,0:T(8,128)} %r_hbm.1, f32[1,1,6,192,192]{4,3,2,1,0:T(8,128)} %s_hbm.1, bf16[1,1,1152,1152]{3,2,1,0:T(8,128)(2,1)} %l_hbm.1, f32[3,16,192]{2,1,0:T(8,128)} %bitcast.1, f32[768,768]{1,0:T(8,128)} %c_hbm.1), custom_call_target="tpu_custom_call" | custom-call | tf_op jit(solution)/shard_map/pallas_call | solution.py:364
  91.4 2.4 %copy.7 = f32[1,1,3,192,512]{4,3,2,1,0:T(8,128)} copy(f32[1,1,3,192,512]{4,3,2,1,0:T(8,128)} %shard_map.55) | data formatting | bytes 2359296

commit v4 on v3

--- a/solution.py
+++ b/solution.py
@@ -12,8 +12,9 @@
 CB = 48
 HALF = 256
 CHUNKS = ((0, 128), (128, 256), (384, 128))
-EARLY = ("n0", "w0")
-DURING = ((0, "n1"), (0, "w1"), (0, "n2"), (0, "w2"), (4, "fw"))
+FIRST = ("n0", "w0")
+EARLY = ("n1", "w1")
+DURING = ((0, "n2"), (0, "w2"), (3, "f1"), (6, "f3"), (9, "f2"))
 AFTER = ("s0", "s1", "s2", "l0", "cp", "cx", "l1", "cf", "l2", "ce")
 MESH = pl.DeviceIdType.MESH
 F32 = jnp.float32
@@ -104,6 +105,24 @@
     lower = ((w_dn, n), (w, n_dn))
     upper = ((w_up, n), (w, n_up))
     s_in = {g: send(spk.at[g], spk_in.at[g], lower[g]) for g in (1, 0)}
+    r_in = {}
+
+    def send_loads(g, k):
+        cols = pl.ds(*CHUNKS[k])
+        r_in[g, k] = send(r_hbm.at[0, 0, 2 * g, :, cols], rr.at[g, :, cols], lower[g])
+
+    def forward(d):
+        z_in[d - 1].wait_recv()
+        block = gath.at[y * 4 + (zl + 4 - d) % 4]
+        for peer in y_peers:
+            y_in.append(send(block, block, peer))
+
+    actions = {f"f{d}": lambda d=d: forward(d) for d in (1, 2, 3)}
+    for k in range(len(CHUNKS)):
+        actions[f"n{k}"] = lambda k=k: send_loads(1, k)
+        actions[f"w{k}"] = lambda k=k: send_loads(0, k)
+    for name in FIRST:
+        actions[name]()
     local[2].start()
     local[3].start()
 
@@ -124,23 +143,6 @@
     z_in = [send(gath.at[w], gath.at[w], peer) for peer in z_peers]
     y_in = [send(gath.at[w], gath.at[w], peer) for peer in y_peers]
 
-    r_in = {}
-
-    def send_loads(g, k):
-        cols = pl.ds(*CHUNKS[k])
-        r_in[g, k] = send(r_hbm.at[0, 0, 2 * g, :, cols], rr.at[g, :, cols], lower[g])
-
-    def forward():
-        for copy, d in zip(z_in, (1, 2, 3)):
-            copy.wait_recv()
-            block = gath.at[y * 4 + (zl + 4 - d) % 4]
-            for peer in y_peers:
-                y_in.append(send(block, block, peer))
-
-    actions = {"fw": forward}
-    for k in range(len(CHUNKS)):
-        actions[f"n{k}"] = lambda k=k: send_loads(1, k)
-        actions[f"w{k}"] = lambda k=k: send_loads(0, k)
     for name in EARLY:
         actions[name]()
 

time: 93.9 us -> 91.6 us (0.976)
  the two profiles are of different devices: /device:TPU:29 before, /device:TPU:65 now
where the time goes in v4:
time: 91.6 us; the launch traced here: 90.7 us
  Pallas kernels  88.3 us (96%)
  local copies, waits for them, and re-layouts  2.36 us (3%)
    pallas_call x1, Pallas kernels, per_device(): pl.pallas_call(kernel, out_shape=jax.ShapeDtypeStruct((1, 1, 3, F, R), F3...  88.3 us
    unnamed x1, local copies, waits for them, and re-layouts  2.36 us

profile of v4, /device:TPU:65, one launch (start us, length us, event | category | flops | bytes accessed | tf_op | source)
XLA Modules:
  0.0 90.7 jit_solution(17542609246602327408)
XLA Ops:
  0.0 88.3 %shard_map.55 = f32[1,1,3,192,512]{4,3,2,1,0:T(8,128)} custom-call(f32[1,1,6,192,512]{4,3,2,1,0:T(8,128)} %r_hbm.1, f32[1,1,6,192,192]{4,3,2,1,0:T(8,128)} %s_hbm.1, bf16[1,1,1152,1152]{3,2,1,0:T(8,128)(2,1)} %l_hbm.1, f32[3,16,192]{2,1,0:T(8,128)} %bitcast.1, f32[768,768]{1,0:T(8,128)} %c_hbm.1), custom_call_target="tpu_custom_call" | custom-call | tf_op jit(solution)/shard_map/pallas_call | solution.py:366
  88.3 2.4 %copy.7 = f32[1,1,3,192,512]{4,3,2,1,0:T(8,128)} copy(f32[1,1,3,192,512]{4,3,2,1,0:T(8,128)} %shard_map.55) | data formatting | bytes 2359296
